TPU v7x, 32 devices: a whole 2x2x4 slice. The times are simulated.
32 devices in a mesh: src: 8 (over z, y), att: 4 (over x, core).
Axes of the slice: x: 2, y: 2, z: 4, core: 2. Of those that a mesh axis runs over, the one named last changes fastest.
Arguments:
- astro: float32 [5, 4096], P(None, 'src'), may hold values from -6 to 6
- attitude: float32 [196608], P('att'), may hold values from -6 to 6
- spline_weights: bfloat16 [2048, 64, 128], P(('src', 'att')), may hold values from -0.75 to 0.75
- source_coeffs: bfloat16 [2048, 5, 128], P(('src', 'att')), may hold values from -2.5 to 2.5
- observations: float32 [2048, 128], P(('src', 'att')), may hold values from -12 to 12
- knot_start: int32 [2048], P(('src', 'att')), may hold values from 0 to 49088
- block_count: int32 [4, 32], P('att', 'src'), may hold values from 1 to 16, as said below
Outputs:
- astro_new: float32 [5, 4096], P(None, 'src')
- attitude_new: float32 [196608], P('att')
Inputs may be any that keep to these rules, and one draw needn't show every extreme that they name: `block_count`: A block's live tiles fill its slots 0 to count - 1 at that owner; the other slots hold entries that no output reads. Some block has all 16 slots live.
All inputs are finite; a program needn't handle non-finite values.
Results may differ from a plain program's by a relative error of at most 0.0003.
Values sent between devices are 32-bit elements; how exact they have to be, the bound alone decides.
A program may use at most 64 MiB of HBM per device.

v0:
```python
import jax
import jax.numpy as jnp
from jax import lax
from jax.sharding import PartitionSpec as P

PASSES = 2
damping = 1.0


def attitude_model(weights, window):
    return jnp.sum(weights.astype(jnp.float32) * window[..., None], axis=-2)


def source_model(coeffs, params):
    return jnp.sum(coeffs.astype(jnp.float32) * params, axis=-2)


def local(astro, attitude, spline_weights, source_coeffs, observations, knot_start, block_count):
    blocks = block_count.shape[1]
    param_count = astro.shape[0]
    block_rows = astro.shape[1] // blocks
    slot_count = spline_weights.shape[0] // blocks
    knot_count = spline_weights.shape[1]
    knot_att = attitude.shape[0]
    weights = spline_weights.reshape(blocks, slot_count, knot_count, block_rows)
    coeffs = source_coeffs.reshape(blocks, slot_count, param_count, block_rows)
    observed = observations.reshape(blocks, slot_count, block_rows)
    starts = knot_start.reshape(blocks, slot_count)
    counts = block_count[0]
    tile_data = (weights, coeffs, observed, starts)
    offsets = jnp.arange(knot_count, dtype=jnp.int32)

    def over_slots(step_fn, totals):
        return step_fn(totals, tile_data, 0)

    def live_mask(slot_first, width):
        slot_ids = slot_first + jnp.arange(width, dtype=jnp.int32)
        return (slot_ids[None, :] < counts[:, None]).astype(jnp.float32)

    def residual(tile_part, slot_first, params, attitude_now):
        part_w, part_c, part_y, part_s = tile_part
        live = live_mask(slot_first, part_w.shape[1])
        window = attitude_now[part_s[..., None] + offsets]
        predicted = source_model(part_c, params[:, None]) + attitude_model(part_w, window)
        return (part_y - predicted) * live[..., None]

    def diag_step(totals, tile_part, slot_first):
        part_w, part_c, part_y, part_s = tile_part
        live = live_mask(slot_first, part_w.shape[1])
        source_sq = jnp.sum(jnp.square(part_c.astype(jnp.float32)) * live[:, :, None, None], axis=1)
        knot_sq = jnp.sum(jnp.square(part_w.astype(jnp.float32)), axis=-1) * live[:, :, None]
        return (source_sq, totals[1].at[part_s[..., None] + offsets].add(knot_sq))

    source_zero = jnp.zeros((blocks, param_count, block_rows), jnp.float32)
    knot_zero = jnp.zeros((knot_att,), jnp.float32)
    source_part, knot_part = over_slots(diag_step, (source_zero, knot_zero))
    source_diag = lax.psum(source_part, "att") + damping
    knot_diag = lax.psum(knot_part, "src") + damping
    params = jnp.transpose(astro.reshape(param_count, blocks, block_rows), (1, 0, 2))
    attitude_now = attitude
    for pass_no in range(PASSES):
        params_old = params
        attitude_old = attitude_now

        def source_step(totals, tile_part, slot_first):
            resid = residual(tile_part, slot_first, params_old, attitude_old)
            return jnp.sum(tile_part[1].astype(jnp.float32) * resid[:, :, None, :], axis=1)

        gradient = over_slots(source_step, source_zero)
        gradient = lax.psum(gradient, "att")
        params = params_old + gradient / source_diag
        params_new = params

        def knot_step(totals, tile_part, slot_first):
            resid = residual(tile_part, slot_first, params_new, attitude_old)
            values = jnp.sum(tile_part[0].astype(jnp.float32) * resid[:, :, None, :], axis=-1)
            return totals.at[tile_part[3][..., None] + offsets].add(values)

        knot_terms = over_slots(knot_step, knot_zero)
        knot_terms = lax.psum(knot_terms, "src")
        attitude_now = attitude_old + knot_terms / knot_diag
    astro_new = jnp.transpose(params, (1, 0, 2)).reshape(param_count, blocks * block_rows)
    return (astro_new, attitude_now)


def solution(mesh):
    placed = (
        P(None, "src"),
        P("att"),
        P(("src", "att"), None, None),
        P(("src", "att"), None, None),
        P(("src", "att"), None),
        P(("src", "att")),
        P("att", "src"),
    )
    return jax.shard_map(
        local, mesh=mesh, in_specs=placed, out_specs=(P(None, "src"), P("att")), check_vma=False
    )
```

profile of v0, /device:TPU:0, one launch (start us, length us, event | category | flops | bytes accessed | tf_op | source)
XLA Modules:
  0.0 318.1 jit_solution(2408341965380640918)
XLA Ops:
  7.2 0.7 fusion.14
  7.9 0.1 reshape.180
  8.0 0.7 add.83
  8.8 0.7 reshape.177
  9.7 19.6 %gather_fusion = f32[4096]{0:T(1024)S(1)} fusion(f32[49152]{0:T(1024)} %param.8, s32[4096]{0:T(1024)S(1)} %broadcast_clamp_fusion), kind=kCustom, calls=%fused_computation | custom fusion | bytes 49152 | tf_op jit(solution)/shard_map/gather | solution.py:43
  29.3 0.7 fusion
  30.0 0.1 copy-done.2
  30.3 0.1 multiply_reduce_fusion.1
  30.4 12.8 %all-reduce.1 = (f32[4,5,128]{2,0,1:T(4,128)S(1)}, f32[4,5,128]{2,0,1:T(4,128)S(1)}) all-reduce(f32[4,5,128]{2,0,1:T(4,128)S(1)} %get-tuple-element.5, f32[4,5,128]{2,0,1:T(4,128)S(1)} %get-tuple-element.4), channel_id=1, replica_groups=mesh['src'=8,'att'=4] {'att'}, use_global_device_ids=true, to_apply=%region_3.0 | all-reduce | flops 5120 | bytes 40960 | tf_op jit(solution)/shard_map/psum | solution.py:70
  43.2 0.1 subtract_multiply_fusion.1
  43.3 1.2 fusion.2
  44.7 29.2 %scatter_custom_fusion = f32[49152]{0:T(1024)} fusion(s32[4096]{0:T(1024)S(1)} %reshape.183, f32[4096]{0:T(1024)S(1)} %reshape.201, f32[]{:T(128)} %constant.4.clone.1), kind=kCustom, calls=%fused_computation.30 | custom fusion | flops 4096 | bytes 196612 | tf_op jit(solution)/shard_map/scatter-add | solution.py:77
  73.9 29.2 %scatter_custom_fusion.1 = f32[49152]{0:T(1024)} fusion(s32[4096]{0:T(1024)S(1)} %reshape.183, f32[4096]{0:T(1024)S(1)} %reshape.209, f32[]{:T(128)} %constant.4.clone.1), kind=kCustom, calls=%fused_computation.28 | custom fusion | flops 4096 | bytes 196612 | tf_op jit(solution)/shard_map/scatter-add | solution.py:52
  103.2 71.9 %all-reduce.7.cloned.1.call-done = (f32[49152]{0:T(1024)}, f32[49152]{0:T(1024)}) async-done(((f32[49152]{0:T(1024)}, f32[49152]{0:T(1024)}), (f32[49152]{0:T(1024)}, f32[49152]{0:T(1024)})) %all-reduce.7.cloned.1.call-update) | async-done | bytes 393232 | tf_op jit(solution)/shard_map/psum | solution.py:80
  175.1 1.1 divide_add_fusion.1
  176.1 23.0 %gather_fusion.1 = f32[4096]{0:T(1024)S(1)} fusion(f32[49152]{0:T(1024)S(1)} %divide_add_fusion.1, s32[4096]{0:T(1024)S(1)} %broadcast_clamp_fusion), kind=kCustom, calls=%fused_computation.1 | custom fusion | bytes 49152 | tf_op jit(solution)/shard_map/gather | solution.py:43
  199.3 0.7 fusion.3
  200.1 10.1 %psum.46 = f32[4,5,128]{2,0,1:T(4,128)S(1)} all-reduce(f32[4,5,128]{2,0,1:T(4,128)S(1)} %multiply_reduce_fusion), channel_id=1, replica_groups=mesh['src'=8,'att'=4] {'att'}, use_global_device_ids=true, to_apply=%region_15.0 | all-reduce | flops 2560 | bytes 20480 | tf_op jit(solution)/shard_map/psum | solution.py:70
  210.3 0.1 subtract_multiply_fusion
  210.4 0.6 fusion.4
  211.0 29.2 %scatter_custom_fusion.2 = f32[49152]{0:T(1024)} fusion(s32[4096]{0:T(1024)S(1)} %reshape.183, f32[4096]{0:T(1024)S(1)} %reshape.217, f32[]{:T(128)} %constant.4.clone.1), kind=kCustom, calls=%fused_computation.26 | custom fusion | flops 4096 | bytes 196612 | tf_op jit(solution)/shard_map/scatter-add | solution.py:77
  240.3 0.6 copy.11
  240.9 68.7 %all-reduce.5.cloned.1.call-done = f32[49152]{0:T(1024)} async-done(((f32[49152]{0:T(1024)}), f32[49152]{0:T(1024)}) %all-reduce.5.cloned.1.call-update) | async-done | bytes 196624 | tf_op jit(solution)/shard_map/psum | solution.py:80
  309.6 1.6 divide_add_fusion
  (32 shorter events, 1.0 us)
Async XLA Ops:
  7.2 167.9 %all-reduce.7.cloned.1.call-start = ((), (), s32[]{:S(2)}) async-start(), calls=%async_computation.1 | async-start | bytes 786432 | tf_op jit(solution)/shard_map/psum | solution.py:80
  9.6 19.7 %copy-start.1 = (bf16[64,64,128]{2,1,0:T(8,128)(2,1)S(1)}, bf16[64,64,128]{2,1,0:T(8,128)(2,1)}, u32[]{:S(2)}) copy-start(bf16[64,64,128]{2,1,0:T(8,128)(2,1)} %param.9) | copy-start | bytes 3145732
  29.2 0.9 copy-start.2
  29.3 0.9 copy-start.4
  43.3 131.8 %copy-start = (f32[49152]{0:T(1024)S(1)}, f32[49152]{0:T(1024)}, u32[]{:S(2)}) copy-start(f32[49152]{0:T(1024)} %param.8) | copy-start | bytes 589828
  103.2 206.4 %all-reduce.5.cloned.1.call-start = ((), (), s32[]{:S(2)}) async-start(), calls=%async_computation | async-start | bytes 393216 | tf_op jit(solution)/shard_map/psum | solution.py:80
  200.0 109.6 %copy-start.3 = (f32[49152]{0:T(1024)S(1)}, f32[49152]{0:T(1024)}, u32[]{:S(2)}) copy-start(f32[49152]{0:T(1024)} %get-tuple-element.7) | copy-start | bytes 589828
Sparse Core Ops, SparseCore 0:
  103.3 71.7 all-reduce.6
  240.4 69.1 all-reduce.4
where the time goes:
time: 318 us
  waiting for transfers between devices  141 us (44%)
  other arithmetic  95 us (30%)
  local copies, waits for them, and re-layouts  45.3 us (14%)
  blocking collectives  22.9 us (7%)
  between operations  14.2 us (4%)
    psum x2, waiting for transfers between devices, local(): knot_terms = lax.psum(knot_terms, 'src')  141 us
    scatter-add x2, other arithmetic, knot_step(): return totals.at[tile_part[3][..., None] + offsets].add(values)  58.5 us
    gather x2, local copies, waits for them, and re-layouts, residual(): window = attitude_now[part_s[..., None] + offsets]  42.6 us
    scatter-add x1, other arithmetic, diag_step(): return (source_sq, totals[1].at[part_s[..., None] + offsets].add(knot_sq))  29.2 us
    psum x2, blocking collectives, local(): gradient = lax.psum(gradient, 'att')  22.9 us
  transfers between devices with their start and end apart: 2, of which 2 were waited for; matrix products, arithmetic and copies ran while one was open for 0% of the time, Pallas kernels for 0%

commit v1 on v0

--- a/solution.py
+++ b/solution.py
@@ -67,7 +67,11 @@
             return jnp.sum(tile_part[1].astype(jnp.float32) * resid[:, :, None, :], axis=1)
 
         gradient = over_slots(source_step, source_zero)
-        gradient = lax.psum(gradient, "att")
+        amount_of = lax.axis_size("att")
+        y1 = gradient
+        for jj in [k for k in (1, 2, 4, 8, 16) if k < amount_of]:
+            y1 = y1 + lax.ppermute(y1, "att", [(d, d ^ jj) for d in range(amount_of)])
+        gradient = y1
         params = params_old + gradient / source_diag
         params_new = params
 

time: 318 us -> 316 us (level)
  blocking collectives: 22.9 us -> 10.1 us
  waiting for transfers between devices: 141 us -> 146 us
  starting transfers between devices: 0.08 us -> 4.86 us
    psum x2 -> x1, blocking collectives: 22.9 us -> 10.1 us  [local(): source_diag = lax.psum(source_part, 'att') + damping]
    ppermute x0 -> x4, starting transfers between devices: none -> 4.78 us  [local(): y1 = y1 + lax.ppermute(y1, 'att', [(d, d ^ jj) for d in range(amount_of)])]
    ppermute x0 -> x4, waiting for transfers between devices: none -> 4.22 us  [local(): y1 = y1 + lax.ppermute(y1, 'att', [(d, d ^ jj) for d in range(amount_of)])]
  transfers between devices with their start and end apart: 2 -> 6, of which waited for: 2 -> 5; matrix products, arithmetic and copies ran while one was open for 0% -> 0% of each run, Pallas kernels for 0% -> 0%
where the time goes in v1:
time: 316 us; the launch traced here: 315 us
  waiting for transfers between devices  146 us (46%)
  other arithmetic  95 us (30%)
  local copies, waits for them, and re-layouts  45.3 us (14%)
  between operations  14.2 us (4%)
  blocking collectives  10.1 us (3%)
  starting transfers between devices  4.86 us (2%)
    psum x2, waiting for transfers between devices, local(): knot_terms = lax.psum(knot_terms, 'src')  142 us
    scatter-add x2, other arithmetic, knot_step(): return totals.at[tile_part[3][..., None] + offsets].add(values)  58.5 us
    gather x2, local copies, waits for them, and re-layouts, residual(): window = attitude_now[part_s[..., None] + offsets]  42.6 us
    scatter-add x1, other arithmetic, diag_step(): return (source_sq, totals[1].at[part_s[..., None] + offsets].add(knot_sq))  29.2 us
    psum x1, blocking collectives, local(): source_diag = lax.psum(source_part, 'att') + damping  10.1 us
  transfers between devices with their start and end apart: 6, of which 5 were waited for; matrix products, arithmetic and copies ran while one was open for 0% of the time, Pallas kernels for 0%

profile of v1, /device:TPU:0, one launch (start us, length us, event | category | flops | bytes accessed | tf_op | source)
XLA Modules:
  0.0 315.2 jit_solution(2229550229278217061)
XLA Ops:
  7.2 0.7 fusion.14
  7.9 0.7 add.160
  8.7 0.7 reshape.177
  9.6 19.6 %gather_fusion = f32[4096]{0:T(1024)S(1)} fusion(f32[49152]{0:T(1024)} %param.8, s32[4096]{0:T(1024)S(1)} %broadcast_clamp_fusion), kind=kCustom, calls=%fused_computation | custom fusion | bytes 49152 | tf_op jit(solution)/shard_map/gather | solution.py:43
  29.3 0.7 fusion
  30.3 0.5 collective-permute-start
  30.9 0.7 collective-permute-done
  31.6 2.8 collective-permute-start.1
  34.5 10.1 %psum.28 = f32[4,5,128]{2,0,1:T(4,128)S(1)} all-reduce(f32[4,5,128]{2,0,1:T(4,128)S(1)} %get-tuple-element.4), channel_id=1, replica_groups=mesh['src'=8,'att'=4] {'att'}, use_global_device_ids=true, to_apply=%region_4.0 | all-reduce | flops 2560 | bytes 20480 | tf_op jit(solution)/shard_map/psum | solution.py:57
  44.7 1.2 fusion.2
  46.1 29.2 %scatter_custom_fusion = f32[49152]{0:T(1024)} fusion(s32[4096]{0:T(1024)S(1)} %reshape.183, f32[4096]{0:T(1024)S(1)} %reshape.201, f32[]{:T(128)} %constant.4.clone.1), kind=kCustom, calls=%fused_computation.30 | custom fusion | flops 4096 | bytes 196612 | tf_op jit(solution)/shard_map/scatter-add | solution.py:81
  75.3 29.2 %scatter_custom_fusion.1 = f32[49152]{0:T(1024)} fusion(s32[4096]{0:T(1024)S(1)} %reshape.183, f32[4096]{0:T(1024)S(1)} %reshape.209, f32[]{:T(128)} %constant.4.clone.1), kind=kCustom, calls=%fused_computation.28 | custom fusion | flops 4096 | bytes 196612 | tf_op jit(solution)/shard_map/scatter-add | solution.py:52
  104.6 72.9 %all-reduce.6.cloned.1.call-done = (f32[49152]{0:T(1024)}, f32[49152]{0:T(1024)}) async-done(((f32[49152]{0:T(1024)}, f32[49152]{0:T(1024)}), (f32[49152]{0:T(1024)}, f32[49152]{0:T(1024)})) %all-reduce.6.cloned.1.call-update) | async-done | bytes 393232 | tf_op jit(solution)/shard_map/psum | solution.py:84
  177.5 1.1 divide_add_fusion.1
  178.5 23.0 %gather_fusion.1 = f32[4096]{0:T(1024)S(1)} fusion(f32[49152]{0:T(1024)S(1)} %divide_add_fusion.1, s32[4096]{0:T(1024)S(1)} %broadcast_clamp_fusion), kind=kCustom, calls=%fused_computation.1 | custom fusion | bytes 49152 | tf_op jit(solution)/shard_map/gather | solution.py:43
  201.6 0.7 fusion.3
  202.6 1.2 collective-permute-done.2
  203.7 1.4 collective-permute-start.3
  205.1 2.3 collective-permute-done.3
  207.5 0.6 fusion.4
  208.2 29.2 %scatter_custom_fusion.2 = f32[49152]{0:T(1024)} fusion(s32[4096]{0:T(1024)S(1)} %reshape.183, f32[4096]{0:T(1024)S(1)} %reshape.217, f32[]{:T(128)} %constant.4.clone.1), kind=kCustom, calls=%fused_computation.26 | custom fusion | flops 4096 | bytes 196612 | tf_op jit(solution)/shard_map/scatter-add | solution.py:81
  237.5 0.6 copy.11
  238.1 68.7 %all-reduce.4.cloned.1.call-done = f32[49152]{0:T(1024)} async-done(((f32[49152]{0:T(1024)}), f32[49152]{0:T(1024)}) %all-reduce.4.cloned.1.call-update) | async-done | bytes 196624 | tf_op jit(solution)/shard_map/psum | solution.py:84
  306.8 1.6 divide_add_fusion
  (41 shorter events, 1.5 us)
Async XLA Ops:
  7.2 170.3 %all-reduce.6.cloned.1.call-start = ((), (), s32[]{:S(2)}) async-start(), calls=%async_computation.1 | async-start | bytes 786432 | tf_op jit(solution)/shard_map/psum | solution.py:84
  9.6 19.7 %copy-start.1 = (bf16[64,64,128]{2,1,0:T(8,128)(2,1)S(1)}, bf16[64,64,128]{2,1,0:T(8,128)(2,1)}, u32[]{:S(2)}) copy-start(bf16[64,64,128]{2,1,0:T(8,128)(2,1)} %param.9) | copy-start | bytes 3145732
  29.2 0.9 copy-start.2
  29.2 0.9 copy-start.4
  30.3 1.4 collective-permute-start
  31.6 12.9 %collective-permute-start.1 = (f32[4,5,128]{2,0,1:T(4,128)S(1)}, f32[4,5,128]{2,0,1:T(4,128)S(1)}, u32[]{:S(2)}, u32[]{:S(2)}) collective-permute-start(f32[4,5,128]{2,0,1:T(4,128)S(1)} %add.166), channel_id=1, source_target_pairs={{0,2},{1,3},{2,0},{3,1},{4,6},{5,7},{6,4},{7,5},{8,10},{9,11},{10,... | collective-permute-start | bytes 30728 | tf_op jit(solution)/shard_map/ppermute | solution.py:73
  44.7 132.8 %copy-start = (f32[49152]{0:T(1024)S(1)}, f32[49152]{0:T(1024)}, u32[]{:S(2)}) copy-start(f32[49152]{0:T(1024)} %param.8) | copy-start | bytes 589828
  104.6 202.2 %all-reduce.4.cloned.1.call-start = ((), (), s32[]{:S(2)}) async-start(), calls=%async_computation | async-start | bytes 393216 | tf_op jit(solution)/shard_map/psum | solution.py:84
  202.4 104.4 %copy-start.3 = (f32[49152]{0:T(1024)S(1)}, f32[49152]{0:T(1024)}, u32[]{:S(2)}) copy-start(f32[49152]{0:T(1024)} %get-tuple-element.7) | copy-start | bytes 589828
  202.5 1.2 collective-permute-start.2
  203.7 3.7 %collective-permute-start.3 = (f32[4,5,128]{2,0,1:T(4,128)S(1)}, f32[4,5,128]{2,0,1:T(4,128)S(1)}, u32[]{:S(2)}, u32[]{:S(2)}) collective-permute-start(f32[4,5,128]{2,0,1:T(4,128)S(1)} %add.176), channel_id=1, source_target_pairs={{0,2},{1,3},{2,0},{3,1},{4,6},{5,7},{6,4},{7,5},{8,10},{9,11},{10,... | collective-permute-start | bytes 30728 | tf_op jit(solution)/shard_map/ppermute | solution.py:73
Sparse Core Ops, SparseCore 0:
  104.7 72.7 all-reduce.5
  237.6 69.1 all-reduce.3
